TPU v7x, 128 devices: a whole 4x4x4 slice. The times are simulated.
128 devices in a mesh: src: 2 (over core), py: 8 (over x, z_hi), pz: 8 (over y, z_lo).
Axes of the slice: x: 4, y: 4, z: 4 (z_hi: 2, z_lo: 2; z = z_hi * 2 + z_lo), core: 2. Of those that a mesh axis runs over, the one named last changes fastest.
Arguments:
- speed: float32 [256, 256, 256], P('pz', 'py'), may hold values from 0.965 to 1.035
- sign_bits: int32 [2, 1024], P('src'), may hold values from 0 to 1
- positions: int32 [3, 1024], replicated, may hold values from 0 to 255
- observed: float32 [2, 2, 256, 256, 256], P('src', None, 'pz', 'py'), may hold values from -3 to 3
Outputs:
- fields: float32 [2, 2, 256, 256, 256], P('src', None, 'pz', 'py')
- gradient: float32 [256, 256, 256], P('pz', 'py', 'src')
All inputs are finite; a program needn't handle non-finite values.
Results may differ from a plain program's by a relative error of at most 0.00022.
Values sent between devices are 32-bit elements; how exact they have to be, the bound alone decides.
A program may use at most 128 MiB of HBM per device.

v0:
```python
import math

import jax
import jax.numpy as jnp
from jax import lax
from jax.sharding import PartitionSpec as P

ITERS = 2


wave_sq = (2.0 * math.pi / 8.0) ** 2
damping = 0.05
source_gain = 40.0
highest = lax.Precision.HIGHEST


def wavenumber(length, start, count):
    freq = start + jnp.arange(count, dtype=jnp.int32)
    signed = jnp.where(freq < length // 2, freq, freq - length)
    return signed.astype(jnp.float32) * (2.0 * math.pi / length)


def green(first, second, third):
    shifted = (
        first[:, None, None] ** 2 + second[None, :, None] ** 2 + third[None, None, :] ** 2 - wave_sq
    )
    denom = shifted * shifted + damping * damping
    return (shifted / denom, damping / denom)


def dft_table(length, inverse):
    counter = jnp.arange(length, dtype=jnp.int32)
    phase = counter[:, None] * counter[None, :] % length
    angle = phase.astype(jnp.float32) * (2.0 * math.pi / length)
    cosine = jnp.cos(angle)
    sine = jnp.sin(angle)
    if inverse:
        scale = 1.0 / length
        return jnp.stack([jnp.stack([cosine, -sine]), jnp.stack([sine, cosine])]) * scale
    return jnp.stack([jnp.stack([cosine, sine]), jnp.stack([-sine, cosine])])


def complex_scale(spectrum, green_re, green_im):
    real_part = spectrum[:, 0]
    imag_part = spectrum[:, 1]
    return jnp.stack(
        [real_part * green_re - imag_part * green_im, real_part * green_im + imag_part * green_re],
        axis=1,
    )


def split_last(block, outer):
    shape = block.shape
    return block.reshape(shape[0], shape[1], shape[2], outer, shape[3] // outer)


def merge_last(block):
    shape = block.shape
    return block.reshape(shape[0], shape[1], shape[2], shape[3] * shape[4])


def via_y(drive, forward, backward, index_y, index_z):
    length = drive.shape[-1]
    count_q = length // lax.axis_size("pz")
    count_k = length // lax.axis_size("py")
    green_re, green_im = green(
        wavenumber(length, 0, length),
        wavenumber(length, index_z * count_q, count_q),
        wavenumber(length, index_y * count_k, count_k),
    )
    sectioned = merge_last(jnp.einsum("dckx,pczyx->pdkyz", forward, drive, precision=highest))
    block = lax.all_to_all(sectioned, "py", split_axis=2, concat_axis=3, tiled=True)
    block = split_last(block, length)
    sectioned = merge_last(jnp.einsum("pckYz,dcqY->pdqzk", block, forward, precision=highest))
    block = lax.all_to_all(sectioned, "pz", split_axis=2, concat_axis=3, tiled=True)
    block = split_last(block, length)
    spectrum = jnp.einsum("pcaZk,dcrZ->pdrak", block, forward, precision=highest)
    spectrum = complex_scale(spectrum, green_re, green_im)
    sectioned = merge_last(jnp.einsum("pdrak,edZr->peaZk", spectrum, backward, precision=highest))
    block = lax.all_to_all(sectioned, "pz", split_axis=3, concat_axis=2, tiled=True)
    block = split_last(block, block.shape[3] // count_k)
    sectioned = merge_last(jnp.einsum("pcqzk,dcYq->pdkYz", block, backward, precision=highest))
    block = lax.all_to_all(sectioned, "py", split_axis=3, concat_axis=2, tiled=True)
    block = split_last(block, block.shape[3] // (length // lax.axis_size("pz")))
    return jnp.einsum("pckyz,dcxk->pdzyx", block, backward, precision=highest)


def per_device(speed, sign_bits, positions, observed):
    patterns = sign_bits.shape[0]
    emitters = sign_bits.shape[1]
    slab_z, slab_y, length = speed.shape
    index_z = lax.axis_index("pz")
    index_y = lax.axis_index("py")
    forward = dft_table(length, False)
    backward = dft_table(length, True)
    local_z = positions[0] - index_z * slab_z
    local_y = positions[1] - index_y * slab_y
    hit_z = (local_z[:, None] == jnp.arange(slab_z, dtype=jnp.int32)[None, :]).astype(jnp.float32)
    hit_y = (local_y[:, None] == jnp.arange(slab_y, dtype=jnp.int32)[None, :]).astype(jnp.float32)
    hit_x = (positions[2][:, None] == jnp.arange(length, dtype=jnp.int32)[None, :]).astype(
        jnp.float32
    )
    plane = (hit_z[:, :, None] * hit_y[:, None, :]).reshape(emitters, slab_z * slab_y)
    weights = (2 * sign_bits - 1).astype(jnp.float32) * source_gain
    weighted = weights[:, :, None] * hit_x[None, :, :]
    source = jnp.einsum("pex,em->pmx", weighted, plane, precision=highest).reshape(
        patterns, slab_z, slab_y, length
    )
    inverse_sq = 1.0 / (speed * speed)
    real_v = wave_sq * (inverse_sq - 1.0)
    ratio = real_v / damping
    field = jnp.zeros((patterns, 2, slab_z, slab_y, length), jnp.float32)
    for step in range(ITERS):
        real_part = field[:, 0]
        imag_part = field[:, 1]
        drive = jnp.stack(
            [
                real_v * real_part + damping * imag_part + source,
                real_v * imag_part - damping * real_part,
            ],
            axis=1,
        )
        spread = via_y(drive, forward, backward, index_y, index_z)
        delta_re = spread[:, 0] - real_part
        delta_im = spread[:, 1] - imag_part
        field = jnp.stack(
            [real_part + delta_re - ratio * delta_im, imag_part + delta_im + ratio * delta_re],
            axis=1,
        )
    misfit_re = field[:, 0] - observed[:, 0]
    misfit_im = field[:, 1] - observed[:, 1]
    partial_term = (
        jnp.sum(misfit_re * field[:, 0] + misfit_im * field[:, 1], axis=0)
        * (-2.0 * wave_sq)
        * inverse_sq
        / speed
    )
    gradient = lax.psum_scatter(partial_term, "src", scatter_dimension=2, tiled=True)
    return (field, gradient)


def solution(mesh):
    return jax.shard_map(
        per_device,
        mesh=mesh,
        in_specs=(P("pz", "py", None), P("src", None), P(), P("src", None, "pz", "py", None)),
        out_specs=(P("src", None, "pz", "py", None), P("pz", "py", "src")),
        check_vma=False,
    )
```

profile of v0, /device:TPU:1, one launch (start us, length us, event | category | flops | bytes accessed | tf_op | source)
XLA Modules:
  0.0 716.5 jit_solution(825033791543685640)
XLA Ops:
  26.9 35.2 %all_to_all.120 = f32[1,2,256,1024]{3,1,0,2:T(2,128)S(1)} all-to-all(f32[1,2,256,1024]{3,1,0,2:T(2,128)} %copy.78), channel_id=1, replica_groups=mesh['src'=2,'py'=8,'pz'=8] {'py'}, dimensions={2} | all-to-all | bytes 4194304 | tf_op jit(solution)/shard_map/all_to_all | solution.py:72
  71.9 17.5 %fusion.45 = f32[1,2,256,32,32]{2,3,4,1,0:T(8,128)S(1)} fusion(f32[2,32,256,32]{3,2,1,0:T(8,128)} %reshape.484, f32[1,2,256,256]{3,2,1,0:T(8,128)S(1)} %get-tuple-element.14, f32[1,2,256,256]{3,2,1,0:T(8,128)S(1)} %get-tuple-element.17), kind=kOutput, calls=%fused_computation.38 | convolution fusion | flops 3221487616 | bytes 5242880 | tf_op jit(solution)/shard_map/pckYz,dcqY->pdqzk/dot_general | solution.py:74
  101.0 28.5 %all-to-all-done.1 = f32[1,2,256,1024]{3,1,0,2:T(2,128)} async-done(((f32[1,2,256,1024]{3,1,0,2:T(2,128)}), f32[1,2,256,1024]{3,1,0,2:T(2,128)}, u32[]{:S(2)}, u32[]{:S(2)}) %all-to-all-start.1) | async-done | bytes 2097184 | tf_op jit(solution)/shard_map/all_to_all | solution.py:75
  140.9 17.5 %fusion.48 = f32[1,2,256,32,32]{2,4,3,1,0:T(8,128)S(1)} fusion(f32[2,32,256,32]{3,2,1,0:T(8,128)} %reshape.486, f32[1,2,256,256]{3,2,1,0:T(8,128)S(1)} %get-tuple-element.14, f32[1,2,256,256]{3,2,1,0:T(8,128)S(1)} %get-tuple-element.17), kind=kOutput, calls=%fused_computation.39 | convolution fusion | flops 3221487616 | bytes 5242880 | tf_op jit(solution)/shard_map/pcaZk,dcrZ->pdrak/dot_general | solution.py:77
  171.9 11.4 %reshape.529 = f32[8,1,65536]{2,1,0:T(1,128)} reshape(f32[8192,1,2,32]{3,2,1,0:T(2,128)} %bitcast.326) | data formatting | bytes 4194304
  183.3 28.7 %all_to_all.121 = f32[8,1,65536]{2,1,0:T(1,128)} all-to-all(f32[8,1,65536]{2,1,0:T(1,128)} %reshape.529), channel_id=1, replica_groups=mesh['src'=2,'py'=8,'pz'=8] {'pz'}, dimensions={0} | all-to-all | bytes 4194304 | tf_op jit(solution)/shard_map/all_to_all | solution.py:80
  212.5 8.5 %reduce = f32[8,65536]{1,0:T(8,128)} reduce(f32[8,1,65536]{2,1,0:T(1,128)} %all_to_all.121, f32[]{:T(128)} %broadcast.532), dimensions={1}, to_apply=%all_to_all.94.reduce_sub_computation | reduce | bytes 4194308 | tf_op jit(solution)/shard_map/all_to_all | solution.py:80
  221.0 11.8 %reshape.530 = f32[8192,1,2,32]{3,2,1,0:T(2,128)} reshape(f32[8,65536]{1,0:T(8,128)} %reduce) | data formatting | bytes 4194304
  232.9 11.6 %copy.90 = f32[1,2,32,8,1024]{4,2,3,1,0:T(8,128)} copy(f32[1,2,32,8,1024]{2,1,4,3,0:T(2,128)} %bitcast.327) | data formatting | bytes 4194304 | tf_op jit(solution)/shard_map/all_to_all | solution.py:80
  263.9 11.0 %copy.147 = f32[1,2,32,256,32]{2,1,4,3,0:T(2,128)} copy(f32[1,2,32,256,32]{3,2,4,1,0:T(8,128)} %fusion.33) | data formatting | bytes 4194304 | tf_op jit(solution)/shard_map/reshape | solution.py:59
  274.9 11.4 %reshape.531 = f32[8,1,65536]{2,1,0:T(1,128)} reshape(f32[8192,1,2,32]{3,2,1,0:T(2,128)} %bitcast.328) | data formatting | bytes 4194304
  286.3 29.3 %all_to_all.122 = f32[8,1,65536]{2,1,0:T(1,128)} all-to-all(f32[8,1,65536]{2,1,0:T(1,128)} %reshape.531), channel_id=1, replica_groups=mesh['src'=2,'py'=8,'pz'=8] {'py'}, dimensions={0} | all-to-all | bytes 4194304 | tf_op jit(solution)/shard_map/all_to_all | solution.py:83
  315.6 8.5 %reduce.1 = f32[8,65536]{1,0:T(8,128)} reduce(f32[8,1,65536]{2,1,0:T(1,128)} %all_to_all.122, f32[]{:T(128)} %broadcast.532), dimensions={1}, to_apply=%all_to_all.97.reduce_sub_computation | reduce | bytes 4194308 | tf_op jit(solution)/shard_map/all_to_all | solution.py:83
  324.1 11.8 %reshape.532 = f32[8192,1,2,32]{3,2,1,0:T(2,128)} reshape(f32[8,65536]{1,0:T(8,128)} %reduce.1) | data formatting | bytes 4194304
  336.0 11.6 %copy.94 = f32[1,2,32,8,1024]{4,2,3,1,0:T(8,128)} copy(f32[1,2,32,8,1024]{2,1,4,3,0:T(2,128)} %bitcast.329) | data formatting | bytes 4194304 | tf_op jit(solution)/shard_map/all_to_all | solution.py:83
  379.1 26.7 %all_to_all.123 = f32[1,2,256,1024]{3,1,0,2:T(2,128)S(1)} all-to-all(f32[1,2,256,1024]{3,1,0,2:T(2,128)} %copy.99), channel_id=1, replica_groups=mesh['src'=2,'py'=8,'pz'=8] {'py'}, dimensions={2} | all-to-all | bytes 4194304 | tf_op jit(solution)/shard_map/all_to_all | solution.py:72
  415.6 17.5 %fusion.51 = f32[1,2,256,32,32]{2,3,4,1,0:T(8,128)S(1)} fusion(f32[2,32,256,32]{3,2,1,0:T(8,128)} %reshape.494, f32[1,2,256,256]{3,2,1,0:T(8,128)S(1)} %get-tuple-element.14, f32[1,2,256,256]{3,2,1,0:T(8,128)S(1)} %get-tuple-element.17), kind=kOutput, calls=%fused_computation.40 | convolution fusion | flops 3221487616 | bytes 5242880 | tf_op jit(solution)/shard_map/pckYz,dcqY->pdqzk/dot_general | solution.py:74
  439.9 23.6 %all_to_all.124 = f32[1,2,256,1024]{3,1,0,2:T(2,128)S(1)} all-to-all(f32[1,2,256,1024]{3,1,0,2:T(2,128)} %copy.104), channel_id=1, replica_groups=mesh['src'=2,'py'=8,'pz'=8] {'pz'}, dimensions={2} | all-to-all | bytes 4194304 | tf_op jit(solution)/shard_map/all_to_all | solution.py:75
  473.1 17.5 %fusion.54 = f32[1,2,256,32,32]{2,4,3,1,0:T(8,128)S(1)} fusion(f32[2,32,256,32]{3,2,1,0:T(8,128)} %reshape.496, f32[1,2,256,256]{3,2,1,0:T(8,128)S(1)} %get-tuple-element.14, f32[1,2,256,256]{3,2,1,0:T(8,128)S(1)} %get-tuple-element.17), kind=kOutput, calls=%fused_computation.41 | convolution fusion | flops 3221487616 | bytes 5242880 | tf_op jit(solution)/shard_map/pcaZk,dcrZ->pdrak/dot_general | solution.py:77
  496.1 8.6 %copy.157 = f32[1,2,32,256,32]{2,1,4,3,0:T(2,128)} copy(f32[1,2,32,256,32]{3,4,2,1,0:T(8,128)} %fusion.39) | data formatting | bytes 4194304 | tf_op jit(solution)/shard_map/reshape | solution.py:59
  504.7 11.4 %reshape.533 = f32[8,1,65536]{2,1,0:T(1,128)} reshape(f32[8192,1,2,32]{3,2,1,0:T(2,128)} %bitcast.331) | data formatting | bytes 4194304
  516.0 22.7 %all_to_all.125 = f32[8,1,65536]{2,1,0:T(1,128)} all-to-all(f32[8,1,65536]{2,1,0:T(1,128)} %reshape.533), channel_id=1, replica_groups=mesh['src'=2,'py'=8,'pz'=8] {'pz'}, dimensions={0} | all-to-all | bytes 4194304 | tf_op jit(solution)/shard_map/all_to_all | solution.py:80
  538.7 8.5 %reduce.2 = f32[8,65536]{1,0:T(8,128)} reduce(f32[8,1,65536]{2,1,0:T(1,128)} %all_to_all.125, f32[]{:T(128)} %broadcast.532), dimensions={1}, to_apply=%all_to_all.106.reduce_sub_computation | reduce | bytes 4194308 | tf_op jit(solution)/shard_map/all_to_all | solution.py:80
  547.3 11.8 %reshape.534 = f32[8192,1,2,32]{3,2,1,0:T(2,128)} reshape(f32[8,65536]{1,0:T(8,128)} %reduce.2) | data formatting | bytes 4194304
  559.1 11.6 %copy.111 = f32[1,2,32,8,1024]{4,2,3,1,0:T(8,128)} copy(f32[1,2,32,8,1024]{2,1,4,3,0:T(2,128)} %bitcast.332) | data formatting | bytes 4194304 | tf_op jit(solution)/shard_map/all_to_all | solution.py:80
  590.1 11.0 %copy.158 = f32[1,2,32,256,32]{2,1,4,3,0:T(2,128)} copy(f32[1,2,32,256,32]{3,2,4,1,0:T(8,128)} %fusion.42) | data formatting | bytes 4194304 | tf_op jit(solution)/shard_map/reshape | solution.py:59
  601.1 11.4 %reshape.535 = f32[8,1,65536]{2,1,0:T(1,128)} reshape(f32[8192,1,2,32]{3,2,1,0:T(2,128)} %bitcast.333) | data formatting | bytes 4194304
  612.5 26.0 %all_to_all.126 = f32[8,1,65536]{2,1,0:T(1,128)} all-to-all(f32[8,1,65536]{2,1,0:T(1,128)} %reshape.535), channel_id=1, replica_groups=mesh['src'=2,'py'=8,'pz'=8] {'py'}, dimensions={0} | all-to-all | bytes 4194304 | tf_op jit(solution)/shard_map/all_to_all | solution.py:83
  638.5 8.5 %reduce.3 = f32[8,65536]{1,0:T(8,128)} reduce(f32[8,1,65536]{2,1,0:T(1,128)} %all_to_all.126, f32[]{:T(128)} %broadcast.532), dimensions={1}, to_apply=%all_to_all.109.reduce_sub_computation | reduce | bytes 4194308 | tf_op jit(solution)/shard_map/all_to_all | solution.py:83
  647.0 11.8 %reshape.536 = f32[8192,1,2,32]{3,2,1,0:T(2,128)} reshape(f32[8,65536]{1,0:T(8,128)} %reduce.3) | data formatting | bytes 4194304
  658.9 11.6 %copy.115 = f32[1,2,32,8,1024]{4,2,3,1,0:T(8,128)} copy(f32[1,2,32,8,1024]{2,1,4,3,0:T(2,128)} %bitcast.334) | data formatting | bytes 4194304 | tf_op jit(solution)/shard_map/all_to_all | solution.py:83
  693.8 15.5 %reduce-scatter.2.cloned.1.call-done = f32[32,32,128]{2,1,0:T(8,128)} async-done(((f32[32,32,256]{2,1,0:T(8,128)}), f32[32,32,128]{2,1,0:T(8,128)}) %reduce-scatter.2.cloned.1.call-update) | async-done | bytes 524304 | tf_op jit(solution)/shard_map/reduce_scatter | solution.py:138
  (74 shorter events, 191.2 us)
Async XLA Ops:
  8.2 7.0 copy-start.2
  15.1 1.0 copy-start.3
  15.1 1.1 copy-start.6
  15.1 1.4 copy-start.7
  96.2 33.3 %all-to-all-start.1 = ((f32[1,2,256,1024]{3,1,0,2:T(2,128)}), f32[1,2,256,1024]{3,1,0,2:T(2,128)}, u32[]{:S(2)}, u32[]{:S(2)}) async-start(f32[1,2,256,1024]{3,1,0,2:T(2,128)} %copy.83), calls=%async_computation.1 | async-start | bytes 4194304 | tf_op jit(solution)/shard_map/all_to_all | solution.py:75
  100.8 608.5 %reduce-scatter.2.cloned.1.call-start = ((), (), s32[]{:S(2)}) async-start(), calls=%async_computation.9 | async-start | bytes 1572864 | tf_op jit(solution)/shard_map/reduce_scatter | solution.py:138
  362.3 5.2 copy-start.4
  367.5 1.4 copy-start
  685.1 5.3 copy-start.1
  685.1 5.3 copy-start.5
Sparse Core Ops, SparseCore 0:
  692.4 16.8 reduce-scatter.1
where the time goes:
time: 730 us; the launch traced here: 716 us
  local copies, waits for them, and re-layouts  303 us (42%)
  blocking collectives  192 us (26%)
  matrix products  114 us (16%)
  other arithmetic  44.1 us (6%)
  waiting for transfers between devices  44 us (6%)
  between operations  14.7 us (2%)
    unnamed x24, local copies, waits for them, and re-layouts  94.7 us
    another operation x12, local copies, waits for them, and re-layouts  81.2 us
    all_to_all x2, blocking collectives, via_y(): lax.all_to_all(sectioned, 'py', split_axis=2, concat_axis=3, tiled=True)  62 us
    reshape x8, local copies, waits for them, and re-layouts, merge_last(): return block.reshape(shape[0], shape[1], shape[2], shape[3] * shape[4])  55.5 us
    all_to_all x2, blocking collectives, via_y(): lax.all_to_all(sectioned, 'py', split_axis=3, concat_axis=2, tiled=True)  55.3 us
    all_to_all x2, blocking collectives, via_y(): lax.all_to_all(sectioned, 'pz', split_axis=3, concat_axis=2, tiled=True)  51.4 us
    dot_general x2, matrix products, via_y(): jnp.einsum('pckYz,dcqY->pdqzk', block, forward, precision=highest)  35.1 us
    dot_general x2, matrix products, via_y(): jnp.einsum('pcaZk,dcrZ->pdrak', block, forward, precision=highest)  35.1 us
  transfers between devices with their start and end apart: 2, of which 2 were waited for; matrix products, arithmetic and copies ran while one was open for 0% of the time, Pallas kernels for 0%

commit v1 on v0

v1 whole, which is shorter than its diff:
```python
import functools
import math

import jax
import jax.numpy as jnp
import numpy as np
from jax import lax
from jax.experimental import pallas as pl
from jax.experimental.pallas import tpu as pltpu
from jax.sharding import PartitionSpec as P

MESH = pl.DeviceIdType.MESH
N = 256
SIDE = 8
CHIPS = SIDE * SIDE
BLOCK = N // SIDE
ROWS = BLOCK * BLOCK
LANES = 128
HALVES = 2
PIECES = 1
TILES = 4 // PIECES
MSG = TILES * 8
ORDER = 27

wave_sq = (2.0 * math.pi / 8.0) ** 2
damping = 0.05
source_gain = 40.0


def tables():
    angle = lambda a, b: 2.0 * np.pi * ((a[:, None] * b[None, :]) % N) / N
    count = np.arange(N)
    chip = np.arange(CHIPS)
    freq = np.stack([2 * chip, (N - 2 * chip) % N, 2 * chip + 1, N - 1 - 2 * chip], 1)
    freq[0, 1] = N // 2
    rows = []
    for half in range(HALVES):
        for member in range(2):
            turn = angle(freq[:, 2 * half + member], count)
            rows.append(np.concatenate([np.cos(turn), np.sin(turn)], 1))
            rows.append(np.concatenate([-np.sin(turn), np.cos(turn)], 1))
    along_x = np.concatenate(rows, 0)
    turn = angle(count, count)
    cosine, sine = np.cos(turn), np.sin(turn)
    along_y = np.block([[cosine, -sine], [sine, cosine]])
    order = z_of_row(count)
    forward = np.concatenate([cosine[:, order], sine[:, order]], 0)
    backward = np.concatenate([cosine[order], sine[order]], 0)
    out = []
    for table in (along_x, along_y, forward, backward):
        high = table.astype(jnp.bfloat16)
        out += [high, (table - high.astype(np.float64)).astype(jnp.bfloat16)]
    return out


def z_of_row(row):
    per = N // PIECES
    piece, rest = row // per, row % per
    s, rest = rest // (16 * TILES), rest % (16 * TILES)
    j, rest = rest // (2 * TILES), rest % (2 * TILES)
    return j * BLOCK + 8 * (piece * TILES) + 4 * rest + s


def split(value):
    high = value.astype(jnp.bfloat16)
    return high, (value - high.astype(jnp.float32)).astype(jnp.bfloat16)


def times(value, high, low):
    first, rest = split(value)
    dot = functools.partial(jnp.dot, preferred_element_type=jnp.float32)
    return dot(first, high) + (dot(first, low) + dot(rest, high))


def times_left(high, low, value):
    first, rest = split(value)
    dot = functools.partial(jnp.dot, preferred_element_type=jnp.float32)
    return dot(high, first) + (dot(low, first) + dot(high, rest))


def swap(parts):
    lane = lax.broadcasted_iota(jnp.int32, parts[0].shape, 1)
    odd, upper = (lane & 32) != 0, (lane & 64) != 0
    mid = []
    for b in (0, 2):
        low, high = parts[b], parts[b + 1]
        mid.append(jnp.where(odd, pltpu.roll(high, 32, 1), low))
        mid.append(jnp.where(odd, high, pltpu.roll(low, 96, 1)))
    out = [None] * 4
    for b in (0, 1):
        low, high = mid[b], mid[b + 2]
        out[b] = jnp.where(upper, pltpu.roll(high, 64, 1), low)
        out[b + 2] = jnp.where(upper, high, pltpu.roll(low, 64, 1))
    return out


def kernel(
    speed_hbm, bits_ref, pos_ref, seen_hbm, xh, xl, yh, yl, fh, fl, bh, bl,
    field_hbm, grad_ref,
    sent, got, acc, first, green, plane, drive_h, drive_l, source, speed, seen, field, term, other,
    send_sem, recv_sem, copy_sem, pair_send, pair_recv,
):
    core, py, pz = lax.axis_index("src"), lax.axis_index("py"), lax.axis_index("pz")
    me = py * SIDE + pz
    X, ZH, Y, ZL = py // 2, py % 2, pz // 2, pz % 2
    Z = 2 * ZH + ZL

    def partner(k):
        o = (k * ORDER) % CHIPS
        x, y, z = (X + o // 16) % 4, (Y + o // 4) % 4, (Z + o) % 4
        return 2 * x + z // 2, 2 * y + z % 2

    barrier = pltpu.get_barrier_semaphore()

    @pl.loop(1, CHIPS)
    def _(k):
        a, b = partner(k)
        pl.semaphore_signal(barrier, inc=1, device_id={"py": a, "pz": b}, device_id_type=MESH)

    pl.semaphore_signal(barrier, inc=1, device_id={"src": 1 - core}, device_id_type=MESH)

    get_speed = pltpu.make_async_copy(speed_hbm, speed, copy_sem.at[0])
    get_seen = pltpu.make_async_copy(seen_hbm, seen, copy_sem.at[1])
    get_speed.start()
    get_seen.start()

    def slot(phase, half, piece):
        return (phase * HALVES + half) * PIECES + piece

    def send(phase, half, piece):
        n = slot(phase, half, piece)
        mine = pl.ds(pl.multiple_of(me * MSG, MSG), MSG)

        @pl.loop(1, CHIPS)
        def _(k):
            a, b = partner(k)
            theirs = pl.ds(pl.multiple_of((a * SIDE + b) * MSG, MSG), MSG)
            pltpu.make_async_remote_copy(
                src_ref=sent.at[n, theirs],
                dst_ref=got.at[n, mine],
                send_sem=send_sem.at[n],
                recv_sem=recv_sem.at[n],
                device_id={"py": a, "pz": b},
                device_id_type=MESH,
            ).start()

        got[n, mine] = sent[n, mine]

    def finish(n, sem):
        everyone = got.at[n, pl.ds(0, (CHIPS - 1) * MSG)]
        pltpu.make_async_copy(everyone, everyone, sem.at[n]).wait()

    def arrive(phase, half, piece):
        finish(slot(phase, half, piece), recv_sem)

    def wave_of(index):
        signed = jnp.where(index < N // 2, index, index - N)
        return signed.astype(jnp.float32) * (2.0 * math.pi / N)

    row_id = lax.broadcasted_iota(jnp.int32, (N, N), 0)
    lane_id = lax.broadcasted_iota(jnp.int32, (N, N), 1)
    base = wave_of(row_id) ** 2 + wave_of(lane_id) ** 2

    def green_of(half, member):
        index = 2 * me + half
        if half == 0 and member == 1:
            index = jnp.where(me == 0, N // 2, index)
        wave = index.astype(jnp.float32) * (2.0 * math.pi / N)
        shifted = base + wave * wave - wave_sq
        scale = (1.0 / N**3) / (shifted * shifted + damping * damping)
        green[2 * half + member, :, 0:N] = shifted * scale
        green[2 * half + member, :, N : 2 * N] = damping * scale

    def spectrum_z(value):
        both = times_left(fh[...], fl[...], value)
        real = both[:N, :N] + both[N:, N:]
        imag = both[:N, N:] - both[N:, :N]
        return real, imag

    def filtered(half, member, real, imag):
        g_re = green[2 * half + member, :, 0:N]
        g_im = green[2 * half + member, :, N : 2 * N]
        plane[member * N : (member + 1) * N, 0:N] = real * g_im + imag * g_re
        plane[member * N : (member + 1) * N, N : 2 * N] = real * g_re - imag * g_im

    def inverse(phase, half):
        plane[...] = times(plane[...], yh[...], yl[...])
        for member in range(2):
            both = times_left(bh[...], bl[...], plane[member * N : (member + 1) * N, :])
            real = both[:N, N:] - both[N:, :N]
            imag = both[:N, :N] + both[N:, N:]
            size = 16 * TILES
            for part, value in ((0, real), (1, imag)):
                for piece in range(PIECES):
                    n = slot(phase, half, piece)
                    for h in range(2):
                        rows = [
                            value[(piece * 4 + s) * size : (piece * 4 + s + 1) * size, h * LANES : (h + 1) * LANES]
                            for s in range(4)
                        ]
                        for b, block in enumerate(swap(rows)):
                            start = (4 * h + b) * SIDE * MSG + 2 * member + part
                            sent[n, pl.ds(start, size, stride=4), :] = block

    def gather(phase, half):
        size = 16 * TILES
        for piece in range(PIECES):
            n = slot(phase, half, piece)
            for member in range(2):
                for part in range(2):
                    for h in range(2):
                        rows = [
                            got[n, pl.ds((4 * h + b) * SIDE * MSG + 2 * member + part, size, stride=4), :]
                            for b in range(4)
                        ]
                        for s, block in enumerate(swap(rows)):
                            at = member * N + (piece * 4 + s) * size
                            plane[at : at + size, part * N + h * LANES : part * N + (h + 1) * LANES] = block

    weight = (2 * bits_ref[...] - 1).astype(jnp.float32) * source_gain
    emitters = weight.shape[1]
    z_at, y_at, x_at = pos_ref[0:1, :], pos_ref[1:2, :], pos_ref[2:3, :]
    ids = lax.broadcasted_iota(jnp.int32, (N, emitters), 0)

    def hits(where, index):
        return jnp.where(where == index, 1.0, 0.0).astype(jnp.bfloat16)

    which = lax.broadcasted_iota(jnp.int32, (8, N), 0)
    turn = lax.broadcasted_iota(jnp.int32, (8, N), 1)
    only = jnp.logical_and(which == 1, me == 0)
    turn = (turn * jnp.where(only, N // 2, 2 * me + which // 2)) & (N - 1)
    shift = jnp.where(jnp.logical_and(which % 2 == 1, jnp.logical_not(only)), math.pi / 2.0, 0.0)
    wave_rows = jnp.cos(turn.astype(jnp.float32) * (2.0 * math.pi / N) - shift)
    wh, wl = split(wave_rows)
    x_hits = hits(x_at, ids)
    phases = jnp.dot(wh, x_hits, preferred_element_type=jnp.float32) + jnp.dot(
        wl, x_hits, preferred_element_type=jnp.float32
    )
    phases = phases * weight
    y_hits = hits(y_at, ids)
    z_equal = z_at == z_of_row(ids)

    nt = (((1,), (1,)), ((), ()))
    for half in range(HALVES):
        for member in range(2):
            row = phases[2 * half + member : 2 * half + member + 1, :]
            high = row.astype(jnp.bfloat16).astype(jnp.float32)
            value = 0.0
            for piece_row in (high, row - high):
                left = jnp.where(z_equal, piece_row, 0.0).astype(jnp.bfloat16)
                value = value + lax.dot_general(left, y_hits, nt, preferred_element_type=jnp.float32)
            plane[member * N : (member + 1) * N, 0:N] = value
        lines = times(plane[:, 0:N], yh[0:N, :], yl[0:N, :])
        one_re, one_im = spectrum_z(lines[:N])
        two_re, two_im = spectrum_z(lines[N:])
        for member in range(2):
            green_of(half, member)
        plus_re, plus_im = one_re + two_im, one_im - two_re
        minus_re, minus_im = one_re - two_im, one_im + two_re
        if half == 0:
            alone = me == 0
            plus_re, plus_im = jnp.where(alone, one_re, plus_re), jnp.where(alone, one_im, plus_im)
            minus_re, minus_im = jnp.where(alone, two_re, minus_re), jnp.where(alone, two_im, minus_im)
        filtered(half, 0, plus_re, plus_im)
        filtered(half, 1, minus_re, minus_im)
        inverse(0, half)
        if half == 0:
            pl.semaphore_wait(barrier, CHIPS)
        for piece in range(PIECES):
            send(0, half, piece)

    local_z, local_y = z_at - pz * BLOCK, y_at - py * BLOCK
    inside = (local_z >= 0) & (local_z < BLOCK) & (local_y >= 0) & (local_y < BLOCK)
    cell = jnp.where(inside, local_z * BLOCK + local_y, -1)
    lines = jnp.where(x_at == ids, weight, 0.0).astype(jnp.bfloat16)

    @pl.loop(0, ROWS // N)
    def _(g):
        at = pl.multiple_of(g * N, N)
        source[pl.ds(at, N), :] = lax.dot_general(
            hits(cell - at, ids), lines, nt, preferred_element_type=jnp.float32
        )

    get_speed.wait()

    def x_inverse(phase, half, piece, tile, r):
        n = slot(phase, half, piece)
        rows = [got[n, pl.ds(tile * 8 + r * 4 + kc, CHIPS, stride=MSG), :] for kc in range(4)]
        return times(jnp.concatenate(rows, 0).T, xh[half * N : (half + 1) * N, :], xl[half * N : (half + 1) * N, :])

    def x_forward(phase, half, piece, tile):
        n = slot(phase, half, piece)
        at = pl.multiple_of((piece * TILES + tile) * N, N)
        high, low = drive_h[pl.ds(at, N), :], drive_l[pl.ds(at, N), :]
        table_h, table_l = xh[half * N : (half + 1) * N, :], xl[half * N : (half + 1) * N, :]
        dot = lambda a, b: lax.dot_general(a, b, nt, preferred_element_type=jnp.float32)
        out = dot(table_h, high) + (dot(table_l, high) + dot(table_h, low))
        for r in range(2):
            for kc in range(4):
                sent[n, pl.ds(tile * 8 + r * 4 + kc, CHIPS, stride=MSG), :] = out[
                    kc * CHIPS : (kc + 1) * CHIPS, r * LANES : (r + 1) * LANES
                ]

    def half_inverse(phase):
        for piece in range(PIECES):
            arrive(phase, 0, piece)

            @pl.loop(0, TILES)
            def _(tile):
                for r in range(2):
                    at = pl.multiple_of((piece * TILES + tile) * N + r * LANES, LANES)
                    acc[pl.ds(at, LANES), :] = x_inverse(phase, 0, piece, tile, r)

    def medium(at):
        v = speed[pl.ds(at, LANES), :]
        inverse_sq = 1.0 / (v * v)
        real_v = wave_sq * (inverse_sq - 1.0)
        return v, inverse_sq, real_v

    half_inverse(0)
    for piece in range(PIECES):
        arrive(0, 1, piece)

        @pl.loop(0, TILES)
        def _(tile):
            for r in range(2):
                at = pl.multiple_of((piece * TILES + tile) * N + r * LANES, LANES)
                here = pl.ds(at, LANES)
                spread = acc[here, :] + x_inverse(0, 1, piece, tile, r)
                spread_re, spread_im = spread[:, :N], spread[:, N:]
                _, _, real_v = medium(at)
                ratio = real_v / damping
                real, imag = spread_re - ratio * spread_im, spread_im + ratio * spread_re
                first[here, 0:N] = real
                first[here, N : 2 * N] = imag
                drive_re = real_v * real + damping * imag + source[here, :]
                drive_im = real_v * imag - damping * real
                for part, value in ((0, drive_re), (1, drive_im)):
                    high, low = split(value)
                    drive_h[here, part * N : (part + 1) * N] = high
                    drive_l[here, part * N : (part + 1) * N] = low
            x_forward(1, 0, piece, tile)

        send(1, 0, piece)
    for piece in range(PIECES):

        @pl.loop(0, TILES)
        def _(tile):
            x_forward(1, 1, piece, tile)

        send(1, 1, piece)

    for half in range(HALVES):
        for piece in range(PIECES):
            arrive(1, half, piece)
        gather(1, half)
        plane[...] = times(plane[...], yh[...], yl[...])
        for member in range(2):
            real, imag = spectrum_z(plane[member * N : (member + 1) * N, :])
            filtered(half, member, real, imag)
        inverse(2, half)
        for piece in range(PIECES):
            send(2, half, piece)

    half_inverse(2)
    get_seen.wait()
    for piece in range(PIECES):
        arrive(2, 1, piece)

        @pl.loop(0, TILES)
        def _(tile):
            for r in range(2):
                at = pl.multiple_of((piece * TILES + tile) * N + r * LANES, LANES)
                here = pl.ds(at, LANES)
                spread = acc[here, :] + x_inverse(2, 1, piece, tile, r)
                was_re, was_im = first[here, 0:N], first[here, N : 2 * N]
                delta_re, delta_im = spread[:, :N] - was_re, spread[:, N:] - was_im
                v, inverse_sq, real_v = medium(at)
                ratio = real_v / damping
                real = was_re + delta_re - ratio * delta_im
                imag = was_im + delta_im + ratio * delta_re
                field[0, here, :] = real
                field[1, here, :] = imag
                misfit = (real - seen[0, here, :]) * real + (imag - seen[1, here, :]) * imag
                part = misfit * (-2.0 * wave_sq) * inverse_sq / v
                term[0, here, :] = part[:, :LANES]
                term[1, here, :] = part[:, LANES:]

    swap_terms = pltpu.make_async_remote_copy(
        src_ref=term.at[1 - core],
        dst_ref=other,
        send_sem=pair_send,
        recv_sem=pair_recv,
        device_id={"src": 1 - core},
        device_id_type=MESH,
    )
    swap_terms.start()
    put_field = pltpu.make_async_copy(field, field_hbm, copy_sem.at[0])
    put_field.start()
    swap_terms.wait()
    grad_ref[...] = term[core] + other[...]
    for n in range(3 * HALVES * PIECES):
        finish(n, send_sem)
    put_field.wait()


def per_device(speed, sign_bits, positions, observed):
    f32, bf16 = jnp.float32, jnp.bfloat16
    anywhere = pl.BlockSpec(memory_space=pl.ANY)
    vmem = pl.BlockSpec(memory_space=pltpu.VMEM)
    slots = 3 * HALVES * PIECES
    field, gradient = pl.pallas_call(
        kernel,
        out_shape=(
            jax.ShapeDtypeStruct((2, ROWS, N), f32),
            jax.ShapeDtypeStruct((ROWS, LANES), f32),
        ),
        in_specs=[anywhere, vmem, vmem, anywhere] + [vmem] * 8,
        out_specs=(anywhere, vmem),
        scratch_shapes=[
            pltpu.VMEM((slots, CHIPS * MSG, LANES), f32),
            pltpu.VMEM((slots, CHIPS * MSG, LANES), f32),
            pltpu.VMEM((ROWS, 2 * N), f32),
            pltpu.VMEM((ROWS, 2 * N), f32),
            pltpu.VMEM((4, N, 2 * N), f32),
            pltpu.VMEM((2 * N, 2 * N), f32),
            pltpu.VMEM((ROWS, 2 * N), bf16),
            pltpu.VMEM((ROWS, 2 * N), bf16),
            pltpu.VMEM((ROWS, N), f32),
            pltpu.VMEM((ROWS, N), f32),
            pltpu.VMEM((2, ROWS, N), f32),
            pltpu.VMEM((2, ROWS, N), f32),
            pltpu.VMEM((2, ROWS, LANES), f32),
            pltpu.VMEM((ROWS, LANES), f32),
            pltpu.SemaphoreType.DMA((slots,)),
            pltpu.SemaphoreType.DMA((slots,)),
            pltpu.SemaphoreType.DMA((2,)),
            pltpu.SemaphoreType.DMA,
            pltpu.SemaphoreType.DMA,
        ],
        compiler_params=pltpu.CompilerParams(
            collective_id=0, has_side_effects=True, vmem_limit_bytes=60 << 20
        ),
    )(
        speed.reshape(ROWS, N),
        sign_bits,
        positions,
        observed.reshape(2, ROWS, N),
        *[jnp.asarray(t) for t in tables()],
    )
    return field.reshape(1, 2, BLOCK, BLOCK, N), gradient.reshape(BLOCK, BLOCK, LANES)


def solution(mesh):
    return jax.shard_map(
        per_device,
        mesh=mesh,
        in_specs=(P("pz", "py", None), P("src", None), P(), P("src", None, "pz", "py", None)),
        out_specs=(P("src", None, "pz", "py", None), P("pz", "py", "src")),
        check_vma=False,
    )
```

time: 730 us -> 107 us (0.15); the launches traced: 716 us -> 107 us
  local copies, waits for them, and re-layouts: 303 us -> 4.01 us
  blocking collectives: 192 us -> 0 us
  matrix products: 114 us -> 0 us
  Pallas kernels: 0 us -> 102 us
  other arithmetic: 44.1 us -> 0 us
  waiting for transfers between devices: 44 us -> 0 us
  between operations: 14.7 us -> 0.65 us
    all_to_all x7 -> x0, blocking collectives: 192 us -> none  [the longest x2 62 us: via_y(): lax.all_to_all(sectioned, 'py', split_axis=2, concat_axis=3, tiled=True)]
    dot_general x13 -> x0, matrix products: 114 us -> none  [the longest x2 35.1 us: via_y(): jnp.einsum('pckYz,dcqY->pdqzk', block, forward, precision=highest)]
    pallas_call x0 -> x1, Pallas kernels: none -> 102 us  [per_device(): pl.pallas_call(kernel, out_shape=(jax.ShapeDtypeStruct((2, ROWS, N), f32)...]
    unnamed x24 -> x4, local copies, waits for them, and re-layouts: 94.7 us -> 4.01 us
    another operation x12 -> x0, local copies, waits for them, and re-layouts: 81.2 us -> none
    all_to_all x13 -> x0, local copies, waits for them, and re-layouts: 61.5 us -> none  [the longest x3 23.8 us: via_y(): lax.all_to_all(sectioned, 'pz', split_axis=3, concat_axis=2, tiled=True)]
    reshape x8 -> x0, local copies, waits for them, and re-layouts: 55.5 us -> none  [merge_last(): return block.reshape(shape[0], shape[1], shape[2], shape[3] * shape[4])]
    all_to_all x4 -> x0, other arithmetic: 34.2 us -> none  [the longest x2 17.1 us: via_y(): lax.all_to_all(sectioned, 'py', split_axis=3, concat_axis=2, tiled=True)]
  transfers between devices with their start and end apart: 2 -> 0, of which waited for: 2 -> 0; matrix products, arithmetic and copies ran while one was open for 0% -> 0% of each run, Pallas kernels for 0% -> 0%
where the time goes in v1:
time: 107 us
  Pallas kernels  102 us (95%)
  local copies, waits for them, and re-layouts  4.01 us (4%)
    pallas_call x1, Pallas kernels, per_device(): pl.pallas_call(kernel, out_shape=(jax.ShapeDtypeStruct((2, ROWS, N), f32)...  102 us
    unnamed x4, local copies, waits for them, and re-layouts  4.01 us

profile of v1, /device:TPU:1, one launch (start us, length us, event | category | flops | bytes accessed | tf_op | source)
XLA Modules:
  0.0 106.6 jit_solution(12471248842649237997)
XLA Ops:
  0.6 102.0 %shard_map.131 = (f32[2,1024,256]{2,1,0:T(8,128)}, f32[1024,128]{1,0:T(8,128)}) custom-call(f32[1024,256]{1,0:T(8,128)} %bitcast.6, s32[1,1024]{1,0:T(1,128)} %bits_ref.1, s32[3,1024]{1,0:T(4,128)} %pos_ref.1, f32[2,1024,256]{2,1,0:T(8,128)} %bitcast.5, bf16[512,512]{1,0:T(8,128)(2,1)} %constant.16.clone.xh, bf16[512,512]{1,0:T(8,128)(2,1)} %constant.17.clone.xl, ...), custom_call_target="tpu_custom_call" | custom-call | tf_op jit(solution)/shard_map/pallas_call | solution.py:412
  102.6 0.0 copy-start
  102.6 3.2 %copy.16 = f32[1,2,32,32,256]{4,3,2,1,0:T(8,128)} copy(f32[1,2,32,32,256]{4,3,2,1,0:T(8,128)} %bitcast.4) | data formatting | bytes 4194304
  105.8 0.0 copy-done
  105.8 0.8 copy.17
Async XLA Ops:
  102.6 3.2 %copy-start = (f32[1024,128]{1,0:T(8,128)S(1)}, f32[1024,128]{1,0:T(8,128)}, u32[]{:S(2)}) copy-start(f32[1024,128]{1,0:T(8,128)} %get-tuple-element.5) | copy-start | bytes 1572868

commit v2 on v1

--- a/solution.py
+++ b/solution.py
@@ -17,7 +17,7 @@
 ROWS = BLOCK * BLOCK
 LANES = 128
 HALVES = 2
-PIECES = 1
+PIECES = 2
 TILES = 4 // PIECES
 MSG = TILES * 8
 ORDER = 27
@@ -47,7 +47,7 @@
     forward = np.concatenate([cosine[:, order], sine[:, order]], 0)
     backward = np.concatenate([cosine[order], sine[order]], 0)
     out = []
-    for table in (along_x, along_y, forward, backward):
+    for table in (along_y, forward, backward, along_x):
         high = table.astype(jnp.bfloat16)
         out += [high, (table - high.astype(np.float64)).astype(jnp.bfloat16)]
     return out
@@ -95,20 +95,20 @@
 
 
 def kernel(
-    speed_hbm, bits_ref, pos_ref, seen_hbm, xh, xl, yh, yl, fh, fl, bh, bl,
-    field_hbm, grad_ref,
-    sent, got, acc, first, green, plane, drive_h, drive_l, source, speed, seen, field, term, other,
-    send_sem, recv_sem, copy_sem, pair_send, pair_recv,
+    speed_hbm, bits_hbm, pos_hbm, seen_hbm, yh_hbm, yl_hbm, fh_hbm, fl_hbm, bh_hbm, bl_hbm, xh_hbm, xl_hbm,
+    field, term, other,
+    bits_ref, pos_ref, yh, yl, fh, fl, bh, bl, xh, xl, sent, got, acc, first, green, plane, drive_h, drive_l, source, speed, seen,
+    send_sem, recv_sem, load_sem, pair_send, pair_recv,
 ):
     core, py, pz = lax.axis_index("src"), lax.axis_index("py"), lax.axis_index("pz")
     me = py * SIDE + pz
-    X, ZH, Y, ZL = py // 2, py % 2, pz // 2, pz % 2
+    X, ZH, Y, ZL = py >> 1, py & 1, pz >> 1, pz & 1
     Z = 2 * ZH + ZL
 
     def partner(k):
-        o = (k * ORDER) % CHIPS
-        x, y, z = (X + o // 16) % 4, (Y + o // 4) % 4, (Z + o) % 4
-        return 2 * x + z // 2, 2 * y + z % 2
+        o = (k * ORDER) & (CHIPS - 1)
+        x, y, z = (X + (o >> 4)) & 3, (Y + (o >> 2)) & 3, (Z + o) & 3
+        return 2 * x + (z >> 1), 2 * y + (z & 1)
 
     barrier = pltpu.get_barrier_semaphore()
 
@@ -119,10 +119,11 @@
 
     pl.semaphore_signal(barrier, inc=1, device_id={"src": 1 - core}, device_id_type=MESH)
 
-    get_speed = pltpu.make_async_copy(speed_hbm, speed, copy_sem.at[0])
-    get_seen = pltpu.make_async_copy(seen_hbm, seen, copy_sem.at[1])
-    get_speed.start()
-    get_seen.start()
+    pairs = ((bits_hbm, bits_ref), (pos_hbm, pos_ref), (yh_hbm, yh), (yl_hbm, yl), (fh_hbm, fh), (fl_hbm, fl), (bh_hbm, bh), (bl_hbm, bl),
+             (xh_hbm, xh), (xl_hbm, xl), (speed_hbm, speed), (seen_hbm, seen))
+    loads = [pltpu.make_async_copy(a, b, load_sem.at[n]) for n, (a, b) in enumerate(pairs)]
+    for load in loads:
+        load.start()
 
     def slot(phase, half, piece):
         return (phase * HALVES + half) * PIECES + piece
@@ -217,6 +218,8 @@
                             at = member * N + (piece * 4 + s) * size
                             plane[at : at + size, part * N + h * LANES : part * N + (h + 1) * LANES] = block
 
+    for load in loads[:2]:
+        load.wait()
     weight = (2 * bits_ref[...] - 1).astype(jnp.float32) * source_gain
     emitters = weight.shape[1]
     z_at, y_at, x_at = pos_ref[0:1, :], pos_ref[1:2, :], pos_ref[2:3, :]
@@ -250,6 +253,9 @@
                 left = jnp.where(z_equal, piece_row, 0.0).astype(jnp.bfloat16)
                 value = value + lax.dot_general(left, y_hits, nt, preferred_element_type=jnp.float32)
             plane[member * N : (member + 1) * N, 0:N] = value
+        if half == 0:
+            for load in loads[2:8]:
+                load.wait()
         lines = times(plane[:, 0:N], yh[0:N, :], yl[0:N, :])
         one_re, one_im = spectrum_z(lines[:N])
         two_re, two_im = spectrum_z(lines[N:])
@@ -281,7 +287,8 @@
             hits(cell - at, ids), lines, nt, preferred_element_type=jnp.float32
         )
 
-    get_speed.wait()
+    for load in loads[8:11]:
+        load.wait()
 
     def x_inverse(phase, half, piece, tile, r):
         n = slot(phase, half, piece)
@@ -363,7 +370,8 @@
             send(2, half, piece)
 
     half_inverse(2)
-    get_seen.wait()
+    loads[11].wait()
+    ends = []
     for piece in range(PIECES):
         arrive(2, 1, piece)
 
@@ -383,25 +391,36 @@
                 field[1, here, :] = imag
                 misfit = (real - seen[0, here, :]) * real + (imag - seen[1, here, :]) * imag
                 part = misfit * (-2.0 * wave_sq) * inverse_sq / v
-                term[0, here, :] = part[:, :LANES]
-                term[1, here, :] = part[:, LANES:]
-
-    swap_terms = pltpu.make_async_remote_copy(
-        src_ref=term.at[1 - core],
-        dst_ref=other,
-        send_sem=pair_send,
-        recv_sem=pair_recv,
-        device_id={"src": 1 - core},
-        device_id_type=MESH,
-    )
-    swap_terms.start()
-    put_field = pltpu.make_async_copy(field, field_hbm, copy_sem.at[0])
-    put_field.start()
-    swap_terms.wait()
-    grad_ref[...] = term[core] + other[...]
+                term[0, here, :] = jnp.where(core == 0, part[:, :LANES], part[:, LANES:])
+                term[1, here, :] = jnp.where(core == 0, part[:, LANES:], part[:, :LANES])
+
+        rows = pl.ds(piece * TILES * N, TILES * N)
+        ends.append(
+            pltpu.make_async_remote_copy(
+                src_ref=term.at[1, rows],
+                dst_ref=other.at[rows],
+                send_sem=pair_send.at[piece],
+                recv_sem=pair_recv.at[piece],
+                device_id={"src": 1 - core},
+                device_id_type=MESH,
+            )
+        )
+        ends[-1].start()
+
     for n in range(3 * HALVES * PIECES):
         finish(n, send_sem)
+    for piece in range(PIECES):
+        ends[piece].wait()
+
+
+def close(field, term, other, field_out, gradient_out, total, sem):
+    put_field = pltpu.make_async_copy(field, field_out, sem.at[0])
+    put_field.start()
+    total[...] = term[0] + other[...]
+    put_total = pltpu.make_async_copy(total, gradient_out, sem.at[1])
+    put_total.start()
     put_field.wait()
+    put_total.wait()
 
 
 def per_device(speed, sign_bits, positions, observed):
@@ -409,15 +428,27 @@
     anywhere = pl.BlockSpec(memory_space=pl.ANY)
     vmem = pl.BlockSpec(memory_space=pltpu.VMEM)
     slots = 3 * HALVES * PIECES
-    field, gradient = pl.pallas_call(
+    in_hbm = lambda a: pltpu.with_memory_space_constraint(a, pltpu.HBM)
+    field, term, other = pl.pallas_call(
         kernel,
         out_shape=(
-            jax.ShapeDtypeStruct((2, ROWS, N), f32),
-            jax.ShapeDtypeStruct((ROWS, LANES), f32),
+            pltpu.VMEM((2, ROWS, N), f32),
+            pltpu.VMEM((2, ROWS, LANES), f32),
+            pltpu.VMEM((ROWS, LANES), f32),
         ),
-        in_specs=[anywhere, vmem, vmem, anywhere] + [vmem] * 8,
-        out_specs=(anywhere, vmem),
+        in_specs=[anywhere] * 12,
+        out_specs=(vmem, vmem, vmem),
         scratch_shapes=[
+            pltpu.VMEM(sign_bits.shape, jnp.int32),
+            pltpu.VMEM(positions.shape, jnp.int32),
+            pltpu.VMEM((2 * N, 2 * N), bf16),
+            pltpu.VMEM((2 * N, 2 * N), bf16),
+            pltpu.VMEM((2 * N, N), bf16),
+            pltpu.VMEM((2 * N, N), bf16),
+            pltpu.VMEM((2 * N, N), bf16),
+            pltpu.VMEM((2 * N, N), bf16),
+            pltpu.VMEM((2 * N, 2 * N), bf16),
+            pltpu.VMEM((2 * N, 2 * N), bf16),
             pltpu.VMEM((slots, CHIPS * MSG, LANES), f32),
             pltpu.VMEM((slots, CHIPS * MSG, LANES), f32),
             pltpu.VMEM((ROWS, 2 * N), f32),
@@ -429,25 +460,36 @@
             pltpu.VMEM((ROWS, N), f32),
             pltpu.VMEM((ROWS, N), f32),
             pltpu.VMEM((2, ROWS, N), f32),
-            pltpu.VMEM((2, ROWS, N), f32),
-            pltpu.VMEM((2, ROWS, LANES), f32),
-            pltpu.VMEM((ROWS, LANES), f32),
             pltpu.SemaphoreType.DMA((slots,)),
             pltpu.SemaphoreType.DMA((slots,)),
-            pltpu.SemaphoreType.DMA((2,)),
-            pltpu.SemaphoreType.DMA,
-            pltpu.SemaphoreType.DMA,
+            pltpu.SemaphoreType.DMA((12,)),
+            pltpu.SemaphoreType.DMA((PIECES,)),
+            pltpu.SemaphoreType.DMA((PIECES,)),
         ],
         compiler_params=pltpu.CompilerParams(
-            collective_id=0, has_side_effects=True, vmem_limit_bytes=60 << 20
+            collective_id=0, has_side_effects=True, vmem_limit_bytes=44 << 20
         ),
     )(
-        speed.reshape(ROWS, N),
-        sign_bits,
-        positions,
-        observed.reshape(2, ROWS, N),
-        *[jnp.asarray(t) for t in tables()],
+        in_hbm(speed.reshape(ROWS, N)),
+        in_hbm(sign_bits),
+        in_hbm(positions),
+        in_hbm(observed.reshape(2, ROWS, N)),
+        *[in_hbm(jnp.asarray(t)) for t in tables()],
     )
+    field, gradient = pl.pallas_call(
+        close,
+        out_shape=(
+            pltpu.HBM((2, ROWS, N), f32),
+            pltpu.HBM((ROWS, LANES), f32),
+        ),
+        in_specs=[anywhere, vmem, vmem],
+        out_specs=(anywhere, anywhere),
+        scratch_shapes=[
+            pltpu.VMEM((ROWS, LANES), f32),
+            pltpu.SemaphoreType.DMA((2,)),
+        ],
+        compiler_params=pltpu.CompilerParams(vmem_limit_bytes=4 << 20),
+    )(*[pltpu.with_memory_space_constraint(a, pltpu.VMEM) for a in (field, term, other)])
     return field.reshape(1, 2, BLOCK, BLOCK, N), gradient.reshape(BLOCK, BLOCK, LANES)
 
 

time: 107 us -> 90.8 us (0.85)
  Pallas kernels: 102 us -> 89.5 us
  local copies, waits for them, and re-layouts: 4.01 us -> 0 us
    pallas_call x1 -> x2, Pallas kernels: 102 us -> 89.5 us  [the longest x1 88 us: per_device(): pl.pallas_call(kernel, out_shape=(pltpu.VMEM((2, ROWS, N), f32), pltpu.VM...]
    unnamed x4 -> x0, local copies, waits for them, and re-layouts: 4.01 us -> none
where the time goes in v2:
time: 90.8 us; the launch traced here: 90.3 us
  Pallas kernels  89.5 us (99%)
    pallas_call x1, Pallas kernels, per_device(): pl.pallas_call(kernel, out_shape=(pltpu.VMEM((2, ROWS, N), f32), pltpu.VM...  88 us

profile of v2, /device:TPU:1, one launch (start us, length us, event | category | flops | bytes accessed | tf_op | source)
XLA Modules:
  0.0 90.3 jit_solution(6814253093635913900)
XLA Ops:
  0.6 88.0 %shard_map.131 = (f32[2,1024,256]{2,1,0:T(8,128)S(1)}, f32[2,1024,128]{2,1,0:T(8,128)S(1)}, f32[1024,128]{1,0:T(8,128)S(1)}) custom-call(f32[1024,256]{1,0:T(8,128)} %bitcast.5, s32[1,1024]{1,0:T(1,128)} %bits_hbm.1, s32[3,1024]{1,0:T(4,128)} %pos_hbm.1, f32[2,1024,256]{2,1,0:T(8,128)} %bitcast.4, bf16[512,512]{1,0:T(8,128)(2,1)} %constant.16.clone.yh_hbm, ...), custom_call_target="tpu_custom_call" | custom-call | tf_op jit(solution)/shard_map/pallas_call | solution.py:432
  88.7 1.5 %shard_map.132 = (f32[2,1024,256]{2,1,0:T(8,128)}, f32[1024,128]{1,0:T(8,128)}) custom-call(f32[2,1024,256]{2,1,0:T(8,128)S(1)} %get-tuple-element.7.field, f32[2,1024,128]{2,1,0:T(8,128)S(1)} %get-tuple-element.8.term, f32[1024,128]{1,0:T(8,128)S(1)} %get-tuple-element.9.other), custom_call_target="tpu_custom_call" | custom-call | tf_op jit(solution)/shard_map/pallas_call | solution.py:479

commit v3 on v2

--- a/solution.py
+++ b/solution.py
@@ -20,7 +20,11 @@
 PIECES = 2
 TILES = 4 // PIECES
 MSG = TILES * 8
-ORDER = 27
+ORDER = [
+    42, 58, 41, 46, 38, 43, 26, 47, 59, 54, 25, 62, 57, 22, 34, 30, 40, 27, 37, 39, 45,
+    10, 31, 53, 61, 23, 6, 44, 11, 33, 29, 55, 50, 24, 14, 36, 21, 63, 35, 9, 56, 18,
+    51, 13, 20, 60, 17, 7, 49, 8, 19, 28, 2, 52, 5, 32, 15, 3, 16, 48, 4, 1, 12,
+]
 
 wave_sq = (2.0 * math.pi / 8.0) ** 2
 damping = 0.05
@@ -105,24 +109,24 @@
     X, ZH, Y, ZL = py >> 1, py & 1, pz >> 1, pz & 1
     Z = 2 * ZH + ZL
 
-    def partner(k):
-        o = (k * ORDER) & (CHIPS - 1)
-        x, y, z = (X + (o >> 4)) & 3, (Y + (o >> 2)) & 3, (Z + o) & 3
+    def partner(o):
+        x, y, z = (X + (o >> 4)) & 3, (Y + ((o >> 2) & 3)) & 3, (Z + (o & 3)) & 3
         return 2 * x + (z >> 1), 2 * y + (z & 1)
-
-    barrier = pltpu.get_barrier_semaphore()
-
-    @pl.loop(1, CHIPS)
-    def _(k):
-        a, b = partner(k)
-        pl.semaphore_signal(barrier, inc=1, device_id={"py": a, "pz": b}, device_id_type=MESH)
-
-    pl.semaphore_signal(barrier, inc=1, device_id={"src": 1 - core}, device_id_type=MESH)
 
     pairs = ((bits_hbm, bits_ref), (pos_hbm, pos_ref), (yh_hbm, yh), (yl_hbm, yl), (fh_hbm, fh), (fl_hbm, fl), (bh_hbm, bh), (bl_hbm, bl),
              (xh_hbm, xh), (xl_hbm, xl), (speed_hbm, speed), (seen_hbm, seen))
     loads = [pltpu.make_async_copy(a, b, load_sem.at[n]) for n, (a, b) in enumerate(pairs)]
-    for load in loads:
+    for load in loads[:2]:
+        load.start()
+    barrier = pltpu.get_barrier_semaphore()
+
+    for o in ORDER:
+        a, b = partner(o)
+        pl.semaphore_signal(barrier, inc=1, device_id={"py": a, "pz": b}, device_id_type=MESH)
+
+    pl.semaphore_signal(barrier, inc=1, device_id={"src": 1 - core}, device_id_type=MESH)
+
+    for load in loads[2:]:
         load.start()
 
     def slot(phase, half, piece):
@@ -132,9 +136,8 @@
         n = slot(phase, half, piece)
         mine = pl.ds(pl.multiple_of(me * MSG, MSG), MSG)
 
-        @pl.loop(1, CHIPS)
-        def _(k):
-            a, b = partner(k)
+        for o in ORDER:
+            a, b = partner(o)
             theirs = pl.ds(pl.multiple_of((a * SIDE + b) * MSG, MSG), MSG)
             pltpu.make_async_remote_copy(
                 src_ref=sent.at[n, theirs],

time: 90.8 us -> 88.5 us (0.975)
  Pallas kernels: 89.5 us -> 87.6 us
    pallas_call x1, Pallas kernels: 88 us -> 86.1 us  [per_device(): pl.pallas_call(kernel, out_shape=(pltpu.VMEM((2, ROWS, N), f32), pltpu.VM...]
where the time goes in v3:
time: 88.5 us; the launch traced here: 88.4 us
  Pallas kernels  87.6 us (99%)
    pallas_call x1, Pallas kernels, per_device(): pl.pallas_call(kernel, out_shape=(pltpu.VMEM((2, ROWS, N), f32), pltpu.VM...  86.1 us

profile of v3, /device:TPU:1, one launch (start us, length us, event | category | flops | bytes accessed | tf_op | source)
XLA Modules:
  0.0 88.4 jit_solution(11985134337672004894)
XLA Ops:
  0.6 86.1 %shard_map.131 = (f32[2,1024,256]{2,1,0:T(8,128)S(1)}, f32[2,1024,128]{2,1,0:T(8,128)S(1)}, f32[1024,128]{1,0:T(8,128)S(1)}) custom-call(f32[1024,256]{1,0:T(8,128)} %bitcast.5, s32[1,1024]{1,0:T(1,128)} %bits_hbm.1, s32[3,1024]{1,0:T(4,128)} %pos_hbm.1, f32[2,1024,256]{2,1,0:T(8,128)} %bitcast.4, bf16[512,512]{1,0:T(8,128)(2,1)} %constant.16.clone.yh_hbm, ...), custom_call_target="tpu_custom_call" | custom-call | tf_op jit(solution)/shard_map/pallas_call | solution.py:435
  86.7 1.5 %shard_map.132 = (f32[2,1024,256]{2,1,0:T(8,128)}, f32[1024,128]{1,0:T(8,128)}) custom-call(f32[2,1024,256]{2,1,0:T(8,128)S(1)} %get-tuple-element.7.field, f32[2,1024,128]{2,1,0:T(8,128)S(1)} %get-tuple-element.8.term, f32[1024,128]{1,0:T(8,128)S(1)} %get-tuple-element.9.other), custom_call_target="tpu_custom_call" | custom-call | tf_op jit(solution)/shard_map/pallas_call | solution.py:482

commit v4 on v3

--- a/solution.py
+++ b/solution.py
@@ -35,8 +35,8 @@
     angle = lambda a, b: 2.0 * np.pi * ((a[:, None] * b[None, :]) % N) / N
     count = np.arange(N)
     chip = np.arange(CHIPS)
-    freq = np.stack([2 * chip, (N - 2 * chip) % N, 2 * chip + 1, N - 1 - 2 * chip], 1)
-    freq[0, 1] = N // 2
+    freq = np.stack([2 * chip + 1, N - 1 - 2 * chip, 2 * chip, (N - 2 * chip) % N], 1)
+    freq[0, 3] = N // 2
     rows = []
     for half in range(HALVES):
         for member in range(2):
@@ -166,8 +166,8 @@
     base = wave_of(row_id) ** 2 + wave_of(lane_id) ** 2
 
     def green_of(half, member):
-        index = 2 * me + half
-        if half == 0 and member == 1:
+        index = 2 * me + 1 - half
+        if half == 1 and member == 1:
             index = jnp.where(me == 0, N // 2, index)
         wave = index.astype(jnp.float32) * (2.0 * math.pi / N)
         shifted = base + wave * wave - wave_sq
@@ -187,24 +187,37 @@
         plane[member * N : (member + 1) * N, 0:N] = real * g_im + imag * g_re
         plane[member * N : (member + 1) * N, N : 2 * N] = real * g_re - imag * g_im
 
-    def inverse(phase, half):
-        plane[...] = times(plane[...], yh[...], yl[...])
+    def inverse_pieces(phase, half, pieces, conjugate):
+        size = 16 * TILES
+        high = 4 * size
+        if len(pieces) == PIECES:
+            table_h, table_l = bh[...], bl[...]
+        else:
+            at = pieces[0] * high
+            table_h = jnp.concatenate([bh[at : at + high, :], bh[N + at : N + at + high, :]], 0)
+            table_l = jnp.concatenate([bl[at : at + high, :], bl[N + at : N + at + high, :]], 0)
+        high = high * len(pieces)
         for member in range(2):
-            both = times_left(bh[...], bl[...], plane[member * N : (member + 1) * N, :])
-            real = both[:N, N:] - both[N:, :N]
-            imag = both[:N, :N] + both[N:, N:]
-            size = 16 * TILES
+            both = times_left(table_h, table_l, plane[member * N : (member + 1) * N, :])
+            real = both[:high, N:] - both[high:, :N]
+            imag = both[:high, :N] + both[high:, N:]
+            if conjugate and member == 0:
+                imag = -imag
             for part, value in ((0, real), (1, imag)):
-                for piece in range(PIECES):
+                for place, piece in enumerate(pieces):
                     n = slot(phase, half, piece)
                     for h in range(2):
                         rows = [
-                            value[(piece * 4 + s) * size : (piece * 4 + s + 1) * size, h * LANES : (h + 1) * LANES]
+                            value[(place * 4 + s) * size : (place * 4 + s + 1) * size, h * LANES : (h + 1) * LANES]
                             for s in range(4)
                         ]
                         for b, block in enumerate(swap(rows)):
                             start = (4 * h + b) * SIDE * MSG + 2 * member + part
                             sent[n, pl.ds(start, size, stride=4), :] = block
+
+    def inverse(phase, half):
+        plane[...] = times(plane[...], yh[...], yl[...])
+        inverse_pieces(phase, half, range(PIECES), False)
 
     def gather(phase, half):
         size = 16 * TILES
@@ -233,8 +246,8 @@
 
     which = lax.broadcasted_iota(jnp.int32, (8, N), 0)
     turn = lax.broadcasted_iota(jnp.int32, (8, N), 1)
-    only = jnp.logical_and(which == 1, me == 0)
-    turn = (turn * jnp.where(only, N // 2, 2 * me + which // 2)) & (N - 1)
+    only = jnp.logical_and(which == 3, me == 0)
+    turn = (turn * jnp.where(only, N // 2, 2 * me + jnp.where(which < 2, 1, 0))) & (N - 1)
     shift = jnp.where(jnp.logical_and(which % 2 == 1, jnp.logical_not(only)), math.pi / 2.0, 0.0)
     wave_rows = jnp.cos(turn.astype(jnp.float32) * (2.0 * math.pi / N) - shift)
     wh, wl = split(wave_rows)
@@ -255,28 +268,36 @@
             for piece_row in (high, row - high):
                 left = jnp.where(z_equal, piece_row, 0.0).astype(jnp.bfloat16)
                 value = value + lax.dot_general(left, y_hits, nt, preferred_element_type=jnp.float32)
-            plane[member * N : (member + 1) * N, 0:N] = value
+            if half == 0:
+                plane[0:N, member * N : (member + 1) * N] = value
+            else:
+                plane[member * N : (member + 1) * N, 0:N] = value
+        for member in range(2):
+            green_of(half, member)
         if half == 0:
             for load in loads[2:8]:
                 load.wait()
-        lines = times(plane[:, 0:N], yh[0:N, :], yl[0:N, :])
-        one_re, one_im = spectrum_z(lines[:N])
-        two_re, two_im = spectrum_z(lines[N:])
-        for member in range(2):
-            green_of(half, member)
-        plus_re, plus_im = one_re + two_im, one_im - two_re
-        minus_re, minus_im = one_re - two_im, one_im + two_re
-        if half == 0:
+            real, imag = spectrum_z(times(plane[0:N, :], yh[...], yl[...]))
+            g_re, g_im = green[0, :, 0:N], green[0, :, N : 2 * N]
+            rr, ii, ri, ir = real * g_re, imag * g_im, real * g_im, imag * g_re
+            plane[0:N, 0:N], plane[0:N, N : 2 * N] = ir - ri, rr + ii
+            plane[N : 2 * N, 0:N], plane[N : 2 * N, N : 2 * N] = ir + ri, rr - ii
+            plane[...] = times(plane[...], yh[...], yl[...])
+            for piece in range(PIECES):
+                inverse_pieces(0, 0, [piece], True)
+                if piece == 0:
+                    pl.semaphore_wait(barrier, CHIPS)
+                send(0, 0, piece)
+        else:
+            lines = times(plane[:, 0:N], yh[0:N, :], yl[0:N, :])
+            one_re, one_im = spectrum_z(lines[:N])
+            two_re, two_im = spectrum_z(lines[N:])
             alone = me == 0
-            plus_re, plus_im = jnp.where(alone, one_re, plus_re), jnp.where(alone, one_im, plus_im)
-            minus_re, minus_im = jnp.where(alone, two_re, minus_re), jnp.where(alone, two_im, minus_im)
-        filtered(half, 0, plus_re, plus_im)
-        filtered(half, 1, minus_re, minus_im)
-        inverse(0, half)
-        if half == 0:
-            pl.semaphore_wait(barrier, CHIPS)
-        for piece in range(PIECES):
-            send(0, half, piece)
+            filtered(1, 0, jnp.where(alone, one_re, one_re + two_im), jnp.where(alone, one_im, one_im - two_re))
+            filtered(1, 1, jnp.where(alone, two_re, one_re - two_im), jnp.where(alone, two_im, one_im + two_re))
+            inverse(0, 1)
+            for piece in range(PIECES):
+                send(0, 1, piece)
 
     local_z, local_y = z_at - pz * BLOCK, y_at - py * BLOCK
     inside = (local_z >= 0) & (local_z < BLOCK) & (local_y >= 0) & (local_y < BLOCK)
@@ -374,7 +395,18 @@
 
     half_inverse(2)
     loads[11].wait()
-    ends = []
+
+    def tell(n):
+        rows = pl.ds(pl.multiple_of(n * N, N), N)
+        return pltpu.make_async_remote_copy(
+            src_ref=term.at[1, rows],
+            dst_ref=other.at[rows],
+            send_sem=pair_send.at[n],
+            recv_sem=pair_recv.at[n],
+            device_id={"src": 1 - core},
+            device_id_type=MESH,
+        )
+
     for piece in range(PIECES):
         arrive(2, 1, piece)
 
@@ -397,23 +429,12 @@
                 term[0, here, :] = jnp.where(core == 0, part[:, :LANES], part[:, LANES:])
                 term[1, here, :] = jnp.where(core == 0, part[:, LANES:], part[:, :LANES])
 
-        rows = pl.ds(piece * TILES * N, TILES * N)
-        ends.append(
-            pltpu.make_async_remote_copy(
-                src_ref=term.at[1, rows],
-                dst_ref=other.at[rows],
-                send_sem=pair_send.at[piece],
-                recv_sem=pair_recv.at[piece],
-                device_id={"src": 1 - core},
-                device_id_type=MESH,
-            )
-        )
-        ends[-1].start()
+            tell(piece * TILES + tile).start()
 
     for n in range(3 * HALVES * PIECES):
         finish(n, send_sem)
-    for piece in range(PIECES):
-        ends[piece].wait()
+    for n in range(ROWS // N):
+        tell(n).wait()
 
 
 def close(field, term, other, field_out, gradient_out, total, sem):
@@ -466,8 +487,8 @@
             pltpu.SemaphoreType.DMA((slots,)),
             pltpu.SemaphoreType.DMA((slots,)),
             pltpu.SemaphoreType.DMA((12,)),
-            pltpu.SemaphoreType.DMA((PIECES,)),
-            pltpu.SemaphoreType.DMA((PIECES,)),
+            pltpu.SemaphoreType.DMA((ROWS // N,)),
+            pltpu.SemaphoreType.DMA((ROWS // N,)),
         ],
         compiler_params=pltpu.CompilerParams(
             collective_id=0, has_side_effects=True, vmem_limit_bytes=44 << 20

time: 88.5 us -> 88.5 us (level)
  no operation moved by 1% of the time
where the time goes in v4:
time: 88.5 us; the launch traced here: 88.3 us
  Pallas kernels  87.5 us (99%)
    pallas_call x1, Pallas kernels, per_device(): pl.pallas_call(kernel, out_shape=(pltpu.VMEM((2, ROWS, N), f32), pltpu.VM...  86 us

profile of v4, /device:TPU:1, one launch (start us, length us, event | category | flops | bytes accessed | tf_op | source)
XLA Modules:
  0.0 88.3 jit_solution(365727871477450851)
XLA Ops:
  0.6 86.0 %shard_map.131 = (f32[2,1024,256]{2,1,0:T(8,128)S(1)}, f32[2,1024,128]{2,1,0:T(8,128)S(1)}, f32[1024,128]{1,0:T(8,128)S(1)}) custom-call(f32[1024,256]{1,0:T(8,128)} %bitcast.5, s32[1,1024]{1,0:T(1,128)} %bits_hbm.1, s32[3,1024]{1,0:T(4,128)} %pos_hbm.1, f32[2,1024,256]{2,1,0:T(8,128)} %bitcast.4, bf16[512,512]{1,0:T(8,128)(2,1)} %constant.16.clone.yh_hbm, ...), custom_call_target="tpu_custom_call" | custom-call | tf_op jit(solution)/shard_map/pallas_call | solution.py:456
  86.6 1.5 %shard_map.132 = (f32[2,1024,256]{2,1,0:T(8,128)}, f32[1024,128]{1,0:T(8,128)}) custom-call(f32[2,1024,256]{2,1,0:T(8,128)S(1)} %get-tuple-element.7.field, f32[2,1024,128]{2,1,0:T(8,128)S(1)} %get-tuple-element.8.term, f32[1024,128]{1,0:T(8,128)S(1)} %get-tuple-element.9.other), custom_call_target="tpu_custom_call" | custom-call | tf_op jit(solution)/shard_map/pallas_call | solution.py:503

commit v5 on v4

--- a/solution.py
+++ b/solution.py
@@ -17,7 +17,7 @@
 ROWS = BLOCK * BLOCK
 LANES = 128
 HALVES = 2
-PIECES = 2
+PIECES = 4
 TILES = 4 // PIECES
 MSG = TILES * 8
 ORDER = [

time: 88.5 us -> 88.2 us (level)
  no operation moved by 1% of the time
where the time goes in v5:
time: 88.2 us; the launch traced here: 88 us
  Pallas kernels  87.2 us (99%)
    pallas_call x1, Pallas kernels, per_device(): pl.pallas_call(kernel, out_shape=(pltpu.VMEM((2, ROWS, N), f32), pltpu.VM...  85.7 us

profile of v5, /device:TPU:1, one launch (start us, length us, event | category | flops | bytes accessed | tf_op | source)
XLA Modules:
  0.0 88.0 jit_solution(10977184383285506786)
XLA Ops:
  0.6 85.7 %shard_map.131 = (f32[2,1024,256]{2,1,0:T(8,128)S(1)}, f32[2,1024,128]{2,1,0:T(8,128)S(1)}, f32[1024,128]{1,0:T(8,128)S(1)}) custom-call(f32[1024,256]{1,0:T(8,128)} %bitcast.5, s32[1,1024]{1,0:T(1,128)} %bits_hbm.1, s32[3,1024]{1,0:T(4,128)} %pos_hbm.1, f32[2,1024,256]{2,1,0:T(8,128)} %bitcast.4, bf16[512,512]{1,0:T(8,128)(2,1)} %constant.16.clone.yh_hbm, ...), custom_call_target="tpu_custom_call" | custom-call | tf_op jit(solution)/shard_map/pallas_call | solution.py:456
  86.4 1.5 %shard_map.132 = (f32[2,1024,256]{2,1,0:T(8,128)}, f32[1024,128]{1,0:T(8,128)}) custom-call(f32[2,1024,256]{2,1,0:T(8,128)S(1)} %get-tuple-element.7.field, f32[2,1024,128]{2,1,0:T(8,128)S(1)} %get-tuple-element.8.term, f32[1024,128]{1,0:T(8,128)S(1)} %get-tuple-element.9.other), custom_call_target="tpu_custom_call" | custom-call | tf_op jit(solution)/shard_map/pallas_call | solution.py:503
